TPU v7x, 32 devices: a whole 2x2x4 slice. The times are simulated.
32 devices in a mesh: dp: 4 (over x, core), fsdp: 8 (over z, y).
Axes of the slice: x: 2, y: 2, z: 4, core: 2. Of those that a mesh axis runs over, the one named last changes fastest.
Arguments:
- tokens: bfloat16 [16384, 768], P(('dp', 'fsdp')), may hold values from -6 to 6
- bucket_len: int32 [32], P(('dp', 'fsdp')), may hold values from 128 to 512, as said below
- valid: int32 [16384], P(('dp', 'fsdp')), may hold values from 0 to 1, as said below
- routes: int32 [16384, 1], P(('dp', 'fsdp')), may hold values from 0 to 3
- attn_gain: bfloat16 [768], P(('dp', 'fsdp')), may hold values from 0.5 to 1.5
- qkv_weight: bfloat16 [768, 2304], P(('dp', 'fsdp')), may hold values from -0.21875 to 0.21875
- out_weight: bfloat16 [768, 768], P(('dp', 'fsdp')), may hold values from -0.875 to 0.875
- relative_head_bias: float32 [12, 32], replicated, may hold values from -4 to 4
- ffn_gain: bfloat16 [768], P(('dp', 'fsdp')), may hold values from 0.5 to 1.5
- router_weight: bfloat16 [768, 4], P(('dp', 'fsdp')), may hold values from -0.15625 to 0.15625
- w_in: bfloat16 [3072, 4, 768], P(('dp', 'fsdp')), may hold values from -0.21875 to 0.21875
- w_out: bfloat16 [3072, 4, 768], P(('dp', 'fsdp')), may hold values from -0.625 to 0.625
- cotangent: bfloat16 [16384, 768], P(('dp', 'fsdp')), may hold values from -6 to 6
Outputs:
- layer_out: bfloat16 [16384, 768], P(('dp', 'fsdp'))
- tokens_grad: bfloat16 [16384, 768], P(('dp', 'fsdp'))
- attn_gain_grad: float32 [768], P(('dp', 'fsdp'))
- qkv_grad: float32 [768, 2304], P(('dp', 'fsdp'))
- out_grad: float32 [768, 768], P(('dp', 'fsdp'))
- rel_bias_grad: float32 [12, 32], replicated
- ffn_gain_grad: float32 [768], P(('dp', 'fsdp'))
- router_weight_gradient: float32 [768, 4], P(('dp', 'fsdp'))
- w_in_grad: float32 [3072, 4, 768], P(('dp', 'fsdp'))
- w_out_grad: float32 [3072, 4, 768], P(('dp', 'fsdp'))
- dispatched: int32 [4], replicated
- dropped: int32 [4], replicated
Inputs may be any that keep to these rules, and one draw needn't show every extreme that they name: `bucket_len`: each block of 512 tokens holds one sequence (512) or 4 sequences of 128; both kinds occur. `valid`: in each sequence the ones form a prefix that covers more than half of it.
All inputs are finite; a program needn't handle non-finite values.
Results may differ from a plain program's by a relative error of at most 0.014.
Values may be sent and summed in bfloat16 or wider, within the bound.
A program may use at most 320 MiB of HBM per device.

v0:
```python
from functools import partial
import math

import jax
import jax.numpy as jnp
from jax import lax
from jax.sharding import PartitionSpec as P

HEADS = 12
BUCKETS = 32
MAXDIST = 128
LONG = 512


epsilon = 1e-06


def bucket_codes(block_span, bucket_count, reach):
    position = jnp.arange(block_span, dtype=jnp.int32)
    offset_grid = position[None, :] - position[:, None]
    distance = jnp.abs(offset_grid)
    halfway = bucket_count // 2
    exact_span = halfway // 2
    distant = jnp.full(offset_grid.shape, exact_span, jnp.int32)
    for number in range(1, halfway - exact_span):
        threshold = math.ceil(
            exact_span * (reach / exact_span) ** (number / (halfway - exact_span))
        )
        distant = distant + (distance >= threshold).astype(jnp.int32)
    return jnp.where(distance < exact_span, distance, distant) + jnp.where(
        offset_grid > 0, halfway, 0
    )


def block_allowed(length, live_block):
    position = jnp.arange(live_block.shape[0], dtype=jnp.int32)
    segment = position // length
    return (segment[:, None] == segment[None, :]) & (live_block[None, :] > 0)


def rms_forward(values, gain_vector):
    inverse = lax.rsqrt(jnp.mean(values * values, axis=-1, keepdims=True) + epsilon)
    normed = values * inverse
    return (normed, inverse, normed * gain_vector)


def rms_backward(normed, inverse, gain_vector, grad_scaled):
    weighted = grad_scaled * gain_vector
    return inverse * (weighted - normed * jnp.mean(weighted * normed, axis=-1, keepdims=True))


def split_heads(block_rows):
    block_span = block_rows.shape[0]
    model_width = block_rows.shape[1] // 3
    head_size = model_width // HEADS
    return tuple(
        (
            block_rows[:, part_index * model_width : (part_index + 1) * model_width].reshape(
                block_span, HEADS, head_size
            )
            for part_index in range(3)
        )
    )


def block_scores(queries, keys_part, complete_position_bias, allowed):
    score_scale = queries.shape[-1] ** (-0.5)
    scores = (
        jnp.einsum("qhd,khd->hqk", queries, keys_part, preferred_element_type=jnp.float32)
        * score_scale
        + complete_position_bias
    )
    return jnp.where(allowed[None], scores, -1e30)


def attend_forward(complete_position_bias, packed):
    block_rows, length, live_block = packed
    queries, keys_part, values_part = split_heads(block_rows)
    scores = block_scores(
        queries, keys_part, complete_position_bias, block_allowed(length, live_block)
    )
    row_peak = jnp.max(scores, axis=-1, keepdims=True)
    exponent = jnp.exp(scores - row_peak)
    row_total = jnp.sum(exponent, axis=-1, keepdims=True)
    weights_low = (exponent / row_total).astype(jnp.bfloat16)
    mixed_rows = jnp.einsum(
        "hqk,khd->qhd", weights_low, values_part, preferred_element_type=jnp.float32
    )
    return (
        mixed_rows.reshape(block_rows.shape[0], -1).astype(jnp.bfloat16),
        (row_peak + jnp.log(row_total))[..., 0],
    )


def attend_backward(complete_position_bias, bucket_indicator, packed):
    block_rows, length, live_block, grad_mixed, log_total = packed
    queries, keys_part, values_part = split_heads(block_rows)
    scores = block_scores(
        queries, keys_part, complete_position_bias, block_allowed(length, live_block)
    )
    probs_full = jnp.exp(scores - log_total[:, :, None])
    grad_heads = grad_mixed.reshape(queries.shape)
    grad_probs = jnp.einsum(
        "qhd,khd->hqk", grad_heads, values_part, preferred_element_type=jnp.float32
    )
    score_gradient_rows = (
        probs_full * (grad_probs - jnp.sum(probs_full * grad_probs, axis=-1, keepdims=True))
    ).astype(jnp.bfloat16)
    score_scale = queries.shape[-1] ** (-0.5)
    grad_queries = (
        jnp.einsum(
            "hqk,khd->qhd", score_gradient_rows, keys_part, preferred_element_type=jnp.float32
        )
        * score_scale
    )
    grad_keys = (
        jnp.einsum("hqk,qhd->khd", score_gradient_rows, queries, preferred_element_type=jnp.float32)
        * score_scale
    )
    grad_values = jnp.einsum(
        "hqk,qhd->khd",
        probs_full.astype(jnp.bfloat16),
        grad_heads,
        preferred_element_type=jnp.float32,
    )
    table_grad = jnp.einsum(
        "wif,nif->wn", score_gradient_rows, bucket_indicator, preferred_element_type=jnp.float32
    )
    block_span = block_rows.shape[0]
    joined = jnp.concatenate(
        [
            grad_queries.reshape(block_span, -1),
            grad_keys.reshape(block_span, -1),
            grad_values.reshape(block_span, -1),
        ],
        axis=1,
    )
    return (joined.astype(jnp.bfloat16), table_grad)


def per_device(
    tokens,
    bucket_len,
    valid,
    routes,
    attn_gain,
    qkv_weight,
    out_weight,
    relative_head_bias,
    ffn_gain,
    router_weight,
    w_in,
    w_out,
    cotangent,
):
    top_probability = lax.Precision.HIGHEST
    gain_attn, weight_qkv, weight_out, gain_ffn, weight_router = (
        lax.all_gather(attn_gain, ("dp", "fsdp"), axis=0, tiled=True),
        lax.all_gather(qkv_weight, ("dp", "fsdp"), axis=0, tiled=True),
        lax.all_gather(out_weight, ("dp", "fsdp"), axis=0, tiled=True),
        lax.all_gather(ffn_gain, ("dp", "fsdp"), axis=0, tiled=True),
        lax.all_gather(router_weight, ("dp", "fsdp"), axis=0, tiled=True),
    )
    expert_in, expert_out = (
        lax.all_gather(w_in, ("dp", "fsdp"), axis=0, tiled=True),
        lax.all_gather(w_out, ("dp", "fsdp"), axis=0, tiled=True),
    )
    token_count, model_width = tokens.shape
    block_total = token_count // LONG
    expert_count = expert_in.shape[1]
    capacity = (5 * token_count + 4 * expert_count - 1) // (4 * expert_count)
    bucket_grid = bucket_codes(LONG, BUCKETS, MAXDIST)
    selected_bucket = bucket_grid[None] == jnp.arange(BUCKETS, dtype=jnp.int32)[:, None, None]
    bucket_indicator = selected_bucket.astype(jnp.bfloat16)
    complete_position_bias = jnp.einsum(
        "eo,ozm->ezm",
        relative_head_bias,
        selected_bucket.astype(jnp.float32),
        precision=top_probability,
    )
    live_blocks = valid.reshape(block_total, LONG)
    rows_in = tokens.astype(jnp.float32)
    normed_one, inverse_one, scaled_one = rms_forward(rows_in, gain_attn.astype(jnp.float32))
    normed_low = scaled_one.astype(jnp.bfloat16)
    qkv_low = jnp.dot(normed_low, weight_qkv, preferred_element_type=jnp.float32).astype(
        jnp.bfloat16
    )
    qkv_blocks = qkv_low.reshape(block_total, LONG, 3 * model_width)
    mixed_blocks, log_totals = lax.map(
        partial(attend_forward, complete_position_bias), (qkv_blocks, bucket_len, live_blocks)
    )
    mixed_low = mixed_blocks.reshape(token_count, model_width)
    hidden = rows_in + jnp.dot(mixed_low, weight_out, preferred_element_type=jnp.float32)
    normed_two, inverse_two, scaled_two = rms_forward(hidden, gain_ffn.astype(jnp.float32))
    normed_two_low = scaled_two.astype(jnp.bfloat16)
    normed_two_full = normed_two_low.astype(jnp.float32)
    router_probs = jax.nn.softmax(
        jnp.dot(normed_two_full, weight_router.astype(jnp.float32), precision=top_probability),
        axis=-1,
    )
    chosen = routes[:, 0]
    route_hot = chosen[:, None] == jnp.arange(expert_count, dtype=jnp.int32)[None, :]
    gate_value = jnp.sum(jnp.where(route_hot, router_probs, 0.0), axis=1)
    surviving_rows = valid > 0
    route_picks = route_hot & surviving_rows[:, None]
    places = jnp.cumsum(route_picks.astype(jnp.int32), axis=0) - 1
    slot_place = jnp.sum(jnp.where(route_picks, places, 0), axis=1)
    kept_rows = surviving_rows & (slot_place < capacity)
    slot_code = jnp.where(kept_rows, chosen * capacity + slot_place, 0)
    slot_match = (
        jnp.arange(expert_count * capacity, dtype=jnp.int32)[:, None]
        == jnp.where(kept_rows, slot_code, -1)[None, :]
    )
    slot_filled = jnp.any(slot_match, axis=1)
    slot_token = jnp.sum(
        jnp.where(slot_match, jnp.arange(token_count, dtype=jnp.int32)[None, :], 0), axis=1
    )
    slot_rows = jnp.where(
        slot_filled[:, None], normed_two_low[slot_token], jnp.zeros((), jnp.bfloat16)
    ).reshape(expert_count, capacity, model_width)
    expert_inner = jnp.einsum(
        "ecd,fed->ecf", slot_rows, expert_in, preferred_element_type=jnp.float32
    )
    active_low = jax.nn.gelu(expert_inner, approximate=True).astype(jnp.bfloat16)
    result_low = (
        jnp.einsum("ecf,fed->ecd", active_low, expert_out, preferred_element_type=jnp.float32)
        .astype(jnp.bfloat16)
        .reshape(expert_count * capacity, model_width)
    )
    returned = jnp.where(kept_rows[:, None], result_low[slot_code].astype(jnp.float32), 0.0)
    layer_out = (hidden + gate_value[:, None] * returned).astype(jnp.bfloat16)
    sent_local = jnp.sum((route_picks & kept_rows[:, None]).astype(jnp.int32), axis=0)
    lost_local = jnp.sum((route_picks & ~kept_rows[:, None]).astype(jnp.int32), axis=0)
    count_sums = lax.psum(jnp.stack([sent_local, lost_local]), ("dp", "fsdp"))
    gain_attn, weight_qkv, weight_out, gain_ffn, weight_router = (
        lax.all_gather(attn_gain, ("dp", "fsdp"), axis=0, tiled=True),
        lax.all_gather(qkv_weight, ("dp", "fsdp"), axis=0, tiled=True),
        lax.all_gather(out_weight, ("dp", "fsdp"), axis=0, tiled=True),
        lax.all_gather(ffn_gain, ("dp", "fsdp"), axis=0, tiled=True),
        lax.all_gather(router_weight, ("dp", "fsdp"), axis=0, tiled=True),
    )
    expert_in, expert_out = (
        lax.all_gather(w_in, ("dp", "fsdp"), axis=0, tiled=True),
        lax.all_gather(w_out, ("dp", "fsdp"), axis=0, tiled=True),
    )
    grad_out = cotangent.astype(jnp.float32)
    grad_gate = jnp.sum(grad_out * returned, axis=1)
    grad_back = gate_value[:, None] * grad_out
    grad_result = (
        jnp.where(slot_filled[:, None], grad_back[slot_token], 0.0)
        .astype(jnp.bfloat16)
        .reshape(expert_count, capacity, model_width)
    )
    grad_active = jnp.einsum(
        "ecd,fed->ecf", grad_result, expert_out, preferred_element_type=jnp.float32
    )
    unused_value, gelu_pullback = jax.vjp(partial(jax.nn.gelu, approximate=True), expert_inner)
    grad_inner = gelu_pullback(grad_active)[0].astype(jnp.bfloat16)
    grad_slots = jnp.einsum(
        "ecf,fed->ecd", grad_inner, expert_in, preferred_element_type=jnp.float32
    ).reshape(expert_count * capacity, model_width)
    grad_normed_two = jnp.where(kept_rows[:, None], grad_slots[slot_code], 0.0)
    grad_probs = jnp.where(route_hot, grad_gate[:, None], 0.0)
    grad_logits = router_probs * (
        grad_probs - jnp.sum(router_probs * grad_probs, axis=1, keepdims=True)
    )
    grad_normed_two = grad_normed_two + jnp.dot(
        grad_logits, weight_router.astype(jnp.float32).T, precision=top_probability
    )
    grad_hidden = (
        rms_backward(normed_two, inverse_two, gain_ffn.astype(jnp.float32), grad_normed_two)
        + grad_out
    )
    grad_hidden_low = grad_hidden.astype(jnp.bfloat16)
    grad_mixed = jnp.dot(grad_hidden_low, weight_out.T, preferred_element_type=jnp.float32).astype(
        jnp.bfloat16
    )
    joined_blocks, table_grads = lax.map(
        partial(attend_backward, complete_position_bias, bucket_indicator),
        (
            qkv_blocks,
            bucket_len,
            live_blocks,
            grad_mixed.reshape(block_total, LONG, model_width),
            log_totals,
        ),
    )
    grad_qkv = joined_blocks.reshape(token_count, 3 * model_width)
    grad_normed_one = jnp.dot(grad_qkv, weight_qkv.T, preferred_element_type=jnp.float32)
    grad_rows = rms_backward(
        normed_one, inverse_one, gain_attn.astype(jnp.float32), grad_normed_one
    )
    tokens_grad = (grad_rows + grad_hidden).astype(jnp.bfloat16)
    table_grad = lax.psum(jnp.sum(table_grads, axis=0), ("dp", "fsdp"))
    attn_term = jnp.sum(grad_normed_one * normed_one, axis=0)
    qkv_term = jnp.dot(normed_low.T, grad_qkv, preferred_element_type=jnp.float32)
    out_term = jnp.dot(mixed_low.T, grad_hidden_low, preferred_element_type=jnp.float32)
    ffn_term = jnp.sum(grad_normed_two * normed_two, axis=0)
    router_term = jnp.dot(normed_two_full.T, grad_logits, precision=top_probability)
    layer_summed = lax.psum_scatter(
        jnp.concatenate(
            [attn_term[:, None], qkv_term, out_term, ffn_term[:, None], router_term], axis=1
        ),
        ("dp", "fsdp"),
        scatter_dimension=0,
        tiled=True,
    )
    out_term = jnp.einsum(
        "ecf,ecd->fed", active_low, grad_result, preferred_element_type=jnp.float32
    )
    in_term = jnp.einsum("ecd,ecf->fed", slot_rows, grad_inner, preferred_element_type=jnp.float32)
    expert_summed = lax.psum_scatter(
        jnp.concatenate([in_term, out_term], axis=1),
        ("dp", "fsdp"),
        scatter_dimension=0,
        tiled=True,
    )
    attn_gain_grad = layer_summed[:, 0]
    qkv_grad = layer_summed[:, 1 : 1 + 3 * model_width]
    out_grad = layer_summed[:, 1 + 3 * model_width : 1 + 4 * model_width]
    ffn_gain_grad = layer_summed[:, 1 + 4 * model_width]
    router_weight_gradient = layer_summed[:, 2 + 4 * model_width :]
    w_in_grad = expert_summed[:, :expert_count]
    w_out_grad = expert_summed[:, expert_count:]
    return (
        layer_out,
        tokens_grad,
        attn_gain_grad,
        qkv_grad,
        out_grad,
        table_grad,
        ffn_gain_grad,
        router_weight_gradient,
        w_in_grad,
        w_out_grad,
        count_sums[0],
        count_sums[1],
    )


def solution(mesh):
    placed = (
        P(("dp", "fsdp"), None),
        P(("dp", "fsdp")),
        P(("dp", "fsdp")),
        P(("dp", "fsdp"), None),
        P(("dp", "fsdp")),
        P(("dp", "fsdp"), None),
        P(("dp", "fsdp"), None),
        P(),
        P(("dp", "fsdp")),
        P(("dp", "fsdp"), None),
        P(("dp", "fsdp"), None, None),
        P(("dp", "fsdp"), None, None),
        P(("dp", "fsdp"), None),
    )
    return jax.shard_map(
        per_device,
        mesh=mesh,
        in_specs=placed,
        out_specs=(
            P(("dp", "fsdp"), None),
            P(("dp", "fsdp"), None),
            P(("dp", "fsdp")),
            P(("dp", "fsdp"), None),
            P(("dp", "fsdp"), None),
            P(),
            P(("dp", "fsdp")),
            P(("dp", "fsdp"), None),
            P(("dp", "fsdp"), None, None),
            P(("dp", "fsdp"), None, None),
            P(),
            P(),
        ),
        check_vma=False,
    )
```

profile of v0, /device:TPU:0, one launch (start us, length us, event | category | flops | bytes accessed | tf_op | source)
XLA Modules:
  0.0 1370.7 jit_solution(2764166081816112336)
XLA Ops:
  15.1 42.1 %all-reduce.3 = (bf16[768]{0:T(1024)(128)(2,1)S(1)}, bf16[768]{0:T(1024)(128)(2,1)S(1)}) all-reduce(bf16[768]{0:T(1024)(128)(2,1)S(1)} %dynamic-update-slice, bf16[768]{0:T(1024)(128)(2,1)S(1)} %dynamic-update-slice.1), channel_id=1, replica_groups=mesh['dp'=4,'fsdp'=8] {'dp','fsdp'}, use_global_device_ids=true, to_apply=%add | all-reduce | flops 1536 | bytes 6144
  64.5 66.2 %all-gather = bf16[32,24,4]{1,2,0:T(4,128)(2,1)S(1)} all-gather(bf16[1,24,4]{1,2,0:T(4,128)(2,1)} %bitcast.123), channel_id=1, replica_groups=mesh['dp'=4,'fsdp'=8] {'dp','fsdp'}, dimensions={0}, use_global_device_ids=true | all-gather | bytes 6336 | tf_op jit(solution)/shard_map/all_gather | solution.py:162
  132.6 13.7 fusion.1
  153.8 15.3 %fusion.97 = (f32[12,512]{1,0:T(8,128)S(1)}, f32[12,512,512]{1,2,0:T(8,128)S(1)}) fusion(f32[512,512,12]{0,2,1:T(8,128)} %fusion.1, bf16[512,12,64]{0,2,1:T(8,128)(2,1)S(1)} %bitcast.100, bf16[512,12,64]{0,2,1:T(8,128)(2,1)S(1)} %bitcast.94, pred[512,512]{0,1:T(8,128)(4,1)S(1)} %compare_and_fusion), kind=kOutput, calls=%fused_computation.161 | convolution fusion | flops 415229952 | bytes 27025408 | tf_op jit(solution)/shard_map/while/body/eval_jaxpr/qhd,khd->hqk/dot_general | solution.py:69
  184.0 73.0 %all-gather.10.cloned.1.call-done = bf16[3072,4,768]{2,0,1:T(8,128)(2,1)} async-done(((bf16[96,4,768]{2,0,1:T(8,128)(2,1)}), bf16[3072,4,768]{2,0,1:T(8,128)(2,1)}) %all-gather.10.cloned.1.call-update) | async-done | bytes 18874384 | tf_op jit(solution)/shard_map/all_gather | solution.py:165
  256.9 12.2 fusion.52
  269.2 114.0 %all-gather.12.cloned.1.call-done = bf16[3072,4,768]{2,0,1:T(8,128)(2,1)} async-done(((bf16[96,4,768]{2,0,1:T(8,128)(2,1)}), bf16[3072,4,768]{2,0,1:T(8,128)(2,1)}) %all-gather.12.cloned.1.call-update) | async-done | bytes 18874384 | tf_op jit(solution)/shard_map/all_gather | solution.py:166
  383.1 12.4 convolution_convert_fusion.1
  405.3 14.7 %fusion.14 = bf16[4,160,3072]{2,1,0:T(8,128)(2,1)} fusion(f32[4,160,3072]{2,1,0:T(8,128)} %fusion.52, bf16[3072,4,768]{2,0,1:T(8,128)(2,1)} %all-gather.12.cloned.1.call-done, bf16[4,160,768]{2,1,0:T(8,128)(2,1)S(1)} %bitcast.102, pred[4,160]{1,0:T(4,128)(4,1)S(1)} %broadcast_in_dim.185), kind=kOutput, calls=%fused_computation.30 | convolution fusion | flops 3059712000 | bytes 31654528 | tf_op jit(solution)/shard_map/ecd,fed->ecf/dot_general | solution.py:254
  420.0 10.8 fusion.99
  447.1 6.8 fusion.32
  453.9 9.0 multiply_reduce_fusion
  462.9 7.4 multiply_convert_fusion
  473.8 5.2 fusion.50
  479.0 4.1 fusion.29
  483.3 12.8 concatenate.12
  497.3 17.2 %convolution_bitcast_fusion.1 = f32[3072,4,768]{2,0,1:T(8,128)} fusion(bf16[4,160,3072]{2,1,0:T(8,128)(2,1)} %fusion.14, bf16[4,160,768]{2,1,0:T(8,128)(2,1)S(1)} %bitcast.97, pred[4,160]{1,0:T(4,128)(4,1)S(1)} %broadcast_in_dim.185), kind=kOutput, calls=%fused_computation.11 | convolution fusion | flops 3020390400 | bytes 42664576 | tf_op jit(solution)/shard_map/ecd,ecf->fed/dot_general | solution.py:311
  514.5 17.7 %convolution_bitcast_fusion = f32[3072,4,768]{2,0,1:T(8,128)} fusion(bf16[4,160,768]{2,1,0:T(8,128)(2,1)S(1)} %bitcast.103, pred[4,160]{1,0:T(4,128)(4,1)S(1)} %broadcast_in_dim.185, f32[4,160,3072]{2,1,0:T(8,128)} %fusion.52), kind=kOutput, calls=%fused_computation.10 | convolution fusion | flops 3038085120 | bytes 46596736 | tf_op jit(solution)/shard_map/ecf,ecd->fed/dot_general | solution.py:308
  532.2 50.1 %pad_maximum_fusion = f32[3072,8,768]{2,0,1:T(8,128)} fusion(f32[3072,4,768]{2,0,1:T(8,128)} %convolution_bitcast_fusion, f32[3072,4,768]{2,0,1:T(8,128)} %convolution_bitcast_fusion.1), kind=kLoop, calls=%fused_computation.4 | loop fusion | flops 18874368 | bytes 150994944 | tf_op jit(solution)/shard_map/concatenate | solution.py:313
  583.2 41.3 %psum.15 = s32[2,4]{1,0:T(2,128)S(1)} all-reduce(s32[2,4]{1,0:T(2,128)S(1)} %pad_add_fusion), channel_id=1, replica_groups=mesh['dp'=4,'fsdp'=8] {'dp','fsdp'}, use_global_device_ids=true, to_apply=%region_24.25 | all-reduce | flops 8 | bytes 64 | tf_op jit(solution)/shard_map/psum | solution.py:234
  625.0 10.2 fusion.37
  635.1 40.2 %psum.14 = f32[12,32]{1,0:T(8,128)} all-reduce(f32[12,32]{1,0:T(8,128)S(1)} %fusion.37), channel_id=1, replica_groups=mesh['dp'=4,'fsdp'=8] {'dp','fsdp'}, use_global_device_ids=true, to_apply=%region_20.21 | all-reduce | flops 384 | bytes 3072 | tf_op jit(solution)/shard_map/psum | solution.py:294
  678.1 13.5 all-reduce.6.cloned.1.call-done
  697.9 660.5 %reduce-scatter.2.cloned.1.call-done = f32[96,8,768]{2,0,1:T(8,128)} async-done(((f32[3072,8,768]{2,0,1:T(8,128)}), f32[96,8,768]{2,0,1:T(8,128)}) %reduce-scatter.2.cloned.1.call-update) | async-done | bytes 2359312 | tf_op jit(solution)/shard_map/reduce_scatter | solution.py:312
  (188 shorter events, 84.6 us)
Async XLA Ops:
  7.2 125.5 %copy-start = (f32[12,32]{1,0:T(8,128)S(1)}, f32[12,32]{1,0:T(8,128)}, u32[]{:S(2)}) copy-start(f32[12,32]{1,0:T(8,128)} %param.20) | copy-start | bytes 4612
  7.2 124.5 %copy-start.19 = (bf16[512,768]{1,0:T(8,128)(2,1)S(1)}, bf16[512,768]{1,0:T(8,128)(2,1)}, u32[]{:S(2)}) copy-start(bf16[512,768]{1,0:T(8,128)(2,1)} %param.13) | copy-start | bytes 2359300
  7.2 139.1 %all-gather.6.cloned.1.call-start = ((), (), s32[]{:S(2)}) async-start(), calls=%async_computation.1 | async-start | bytes 3649536 | tf_op jit(solution)/shard_map/all_gather | solution.py:159
  7.9 168.2 %all-gather.8.cloned.1.call-start = ((), (), s32[]{:S(2)}) async-start(), calls=%async_computation.2 | async-start | bytes 1216512 | tf_op jit(solution)/shard_map/all_gather | solution.py:160
  8.7 248.2 %all-gather.10.cloned.1.call-start = ((), (), s32[]{:S(2)}) async-start(), calls=%async_computation.3 | async-start | bytes 19464192 | tf_op jit(solution)/shard_map/all_gather | solution.py:165
  10.7 372.4 %all-gather.12.cloned.1.call-start = ((), (), s32[]{:S(2)}) async-start(), calls=%async_computation.4 | async-start | bytes 19464192 | tf_op jit(solution)/shard_map/all_gather | solution.py:166
  12.7 678.9 %all-reduce.6.cloned.1.call-start = ((), (), s32[]{:S(2)}) async-start(), calls=%async_computation.6 | async-start | bytes 19660800
  57.2 89.1 %copy-start.36 = (f32[768]{0:T(1024)}, f32[768]{0:T(1024)S(1)}, u32[]{:S(2)}) copy-start(f32[768]{0:T(1024)S(1)} %convert_element_type.155) | copy-start | bytes 9220
  63.5 334.9 %copy-start.32 = (pred[512]{0:T(512)(128)(4,1)}, pred[512]{0:T(512)(128)(4,1)S(1)}, u32[]{:S(2)}) copy-start(pred[512]{0:T(512)(128)(4,1)S(1)} %get-tuple-element.124) | copy-start | bytes 1540
  130.8 52.1 %copy-start.27 = (bf16[768,4]{0,1:T(4,128)(2,1)}, bf16[768,4]{0,1:T(4,128)(2,1)S(1)}, u32[]{:S(2)}) copy-start(bf16[768,4]{0,1:T(4,128)(2,1)S(1)} %reshape.344) | copy-start | bytes 18436
  131.2 264.4 %copy-start.38 = (s32[1024]{0:T(1024)}, s32[1024]{0:T(1024)S(1)}, u32[]{:S(2)}) copy-start(s32[1024]{0:T(1024)S(1)} %pad_clamp_fusion) | copy-start | bytes 12292
  131.9 14.4 %copy-start.39 = (f32[512]{0:T(512)}, f32[512]{0:T(512)S(1)}, u32[]{:S(2)}) copy-start(f32[512]{0:T(512)S(1)} %add_rsqrt_fusion.1) | copy-start | bytes 6148
  152.1 17.1 %copy-start.8 = (bf16[512,768]{0,1:T(8,128)(2,1)}, bf16[512,768]{0,1:T(8,128)(2,1)S(1)}, u32[]{:S(2)}) copy-start(bf16[512,768]{0,1:T(8,128)(2,1)S(1)} %copy.92) | copy-start | bytes 2359300
  153.8 17.2 %copy-start.17 = (bf16[512,768]{0,1:T(8,128)(2,1)}, bf16[512,768]{0,1:T(8,128)(2,1)S(1)}, u32[]{:S(2)}) copy-start(bf16[512,768]{0,1:T(8,128)(2,1)S(1)} %copy.91) | copy-start | bytes 2359300
  183.0 86.2 %copy-start.6 = (bf16[640,768]{1,0:T(8,128)(2,1)}, bf16[640,768]{1,0:T(8,128)(2,1)S(1)}, u32[]{:S(2)}) copy-start(bf16[640,768]{1,0:T(8,128)(2,1)S(1)} %gather_fusion) | copy-start | bytes 2949124
  447.1 15.8 %slice-start = ((s8[12582912]{0:T(1024)(128)(4,1)}), s8[4194304]{0:T(1024)(128)(4,1)S(1)}, s32[]{:S(2)}) async-start(s8[12582912]{0:T(1024)(128)(4,1)} %bitcast.90), calls=%async_computation.7 | async-start | bytes 8388608
  447.1 15.8 %slice-start.1 = ((s8[12582912]{0:T(1024)(128)(4,1)}), s8[4194304]{0:T(1024)(128)(4,1)S(1)}, s32[]{:S(2)}) async-start(s8[12582912]{0:T(1024)(128)(4,1)} %bitcast.90), calls=%async_computation.8 | async-start | bytes 8388608
  453.9 9.0 slice-start.2
  496.1 18.3 %copy-start.16 = (bf16[640,768]{1,0:T(8,128)(2,1)S(1)}, bf16[640,768]{1,0:T(8,128)(2,1)}, u32[]{:S(2)}) copy-start(bf16[640,768]{1,0:T(8,128)(2,1)} %copy-done.15) | copy-start | bytes 2949124
  496.1 862.2 %reduce-scatter.2.cloned.1.call-start = ((), (), s32[]{:S(2)}) async-start(), calls=%async_computation.5 | async-start | bytes 77856768 | tf_op jit(solution)/shard_map/reduce_scatter | solution.py:312
  582.3 42.7 %copy-start.14 = (s32[512,512]{0,1:T(8,128)S(1)}, s32[512,512]{0,1:T(8,128)}, u32[]{:S(2)}) copy-start(s32[512,512]{0,1:T(8,128)} %copy-done.13) | copy-start | bytes 3145732
  625.0 50.4 %copy-start.42 = (f32[512]{0:T(512)S(1)}, f32[512]{0:T(512)}, u32[]{:S(2)}) copy-start(f32[512]{0:T(512)} %get-tuple-element.116) | copy-start | bytes 6148
  625.0 50.4 %copy-start.21 = (bf16[512,768]{1,0:T(8,128)(2,1)S(1)}, bf16[512,768]{1,0:T(8,128)(2,1)}, u32[]{:S(2)}) copy-start(bf16[512,768]{1,0:T(8,128)(2,1)} %param.13) | copy-start | bytes 2359300
  696.4 667.2 %copy-start.1 = (f32[12,32]{1,0:T(8,128)S(1)}, f32[12,32]{1,0:T(8,128)}, u32[]{:S(2)}) copy-start(f32[12,32]{1,0:T(8,128)} %param.20) | copy-start | bytes 4612
  (31 other events, 110.2 us)
Sparse Core Ops, SparseCore 0:
  11.0 62.9 all-gather.5
  76.8 52.8 all-gather.7
  133.2 123.6 all-gather.9
  260.2 122.8 all-gather.11
  496.2 195.3 all-reduce.5
  699.1 659.2 reduce-scatter.1
where the time goes:
time: 1380 us; the launch traced here: 1370 us
  waiting for transfers between devices  862 us (62%)
  blocking collectives  190 us (14%)
  matrix products  172 us (12%)
  other arithmetic  75.9 us (6%)
  local copies, waits for them, and re-layouts  54.4 us (4%)
  between operations  15.7 us (1%)
    reduce_scatter x1, waiting for transfers between devices, per_device(): lax.psum_scatter(jnp.concatenate([in_term, out_term], axis=1), ('dp', 'fs...  660 us
    all_gather x1, waiting for transfers between devices, per_device(): lax.all_gather(w_out, ('dp', 'fsdp'), axis=0, tiled=True)  114 us
    all_gather x1, waiting for transfers between devices, per_device(): lax.all_gather(w_in, ('dp', 'fsdp'), axis=0, tiled=True)  73 us
    all_gather x1, blocking collectives, per_device(): lax.all_gather(router_weight, ('dp', 'fsdp'), axis=0, tiled=True)  66.2 us
    concatenate x1, other arithmetic, per_device(): jnp.concatenate([in_term, out_term], axis=1)  50.1 us
    unnamed x1, blocking collectives  42.1 us
    psum x1, blocking collectives, per_device(): count_sums = lax.psum(jnp.stack([sent_local, lost_local]), ('dp', 'fsdp'))  41.3 us
    psum x1, blocking collectives, per_device(): table_grad = lax.psum(jnp.sum(table_grads, axis=0), ('dp', 'fsdp'))  40.2 us
  transfers between devices with their start and end apart: 6, of which 4 were waited for; matrix products, arithmetic and copies ran while one was open for 13% of the time, Pallas kernels for 0%

commit v1 on v0

--- a/solution.py
+++ b/solution.py
@@ -4,12 +4,851 @@
 import jax
 import jax.numpy as jnp
 from jax import lax
+from jax.experimental import pallas as pl
+from jax.experimental.pallas import tpu as pltpu
 from jax.sharding import PartitionSpec as P
+
+F32 = jnp.float32
+BF16 = jnp.bfloat16
+MESH = pl.DeviceIdType.MESH
 
 HEADS = 12
 BUCKETS = 32
 MAXDIST = 128
 LONG = 512
+NEG = -1e30
+EPS = 1e-06
+GELU_C = math.sqrt(2.0 / math.pi)
+
+
+def nt(a, b):
+    return lax.dot_general(a, b, (((1,), (1,)), ((), ())), preferred_element_type=F32)
+
+
+def nn(a, b):
+    return lax.dot_general(a, b, (((1,), (0,)), ((), ())), preferred_element_type=F32)
+
+
+def tn(a, b):
+    return lax.dot_general(a, b, (((0,), (0,)), ((), ())), preferred_element_type=F32)
+
+
+def exact(a, b, dims):
+    return lax.dot_general(
+        a, b, (dims, ((), ())), precision=lax.Precision.HIGHEST, preferred_element_type=F32
+    )
+
+
+def iota(shape, axis):
+    return lax.broadcasted_iota(jnp.int32, shape, axis)
+
+
+def bucket_of(offset):
+    distance = jnp.abs(offset)
+    halfway = BUCKETS // 2
+    exact_span = halfway // 2
+    distant = jnp.full(offset.shape, exact_span, jnp.int32)
+    for number in range(1, halfway - exact_span):
+        threshold = math.ceil(
+            exact_span * (MAXDIST / exact_span) ** (number / (halfway - exact_span))
+        )
+        distant = distant + jnp.where(distance >= threshold, 1, 0)
+    return jnp.where(distance < exact_span, distance, distant) + jnp.where(offset > 0, halfway, 0)
+
+
+def diagonal_sums(tile):
+    wide = jnp.concatenate([tile, jnp.zeros((128, 128), F32)], axis=1)
+    rows = 64
+    while rows >= 8:
+        wide = wide[:rows] + pltpu.roll(wide[rows : 2 * rows], 256 - rows, 1)
+        rows //= 2
+    while rows >= 1:
+        wide = wide + pltpu.roll(pltpu.roll(wide, 256 - rows, 1), 8 - rows, 0)
+        rows //= 2
+    return wide[0:1]
+
+
+VMEM_LIMIT = 63 << 20
+
+
+def layer_kernel(
+    tok, cot, routes, valid, length, rel, qshard, oshard, sshard, wi_hbm, wo_hbm,
+    layer_out, tokens_grad, qkv_grad, out_grad, small_grad, wi_grad, wo_grad, p_hbm,
+    aq, ar, wq, wo, sm_t, wb, xg, ycore, yx, ry, rz,
+    qkvb, u1, obuf, u2, gobuf, hid, prob, code_row, cols, key_mask, tab, bias, pst, dst_s, gd, relg,
+    smallp, lsc, lsx, lsy, lsz, fin,
+    free,
+    s1s, s1r, s3zs, s3ys, s3r, s3l, xs, xr, ycs, ycr, yxs, yxr, dys, dyr, dzs, dzr,
+    rcs, rcr, rxs, rxr, rys, ryr, rzs, rzr, psem, fsem,
+):
+    dp = lax.axis_index("dp")
+    fs = lax.axis_index("fsdp")
+    x, c = dp // 2, lax.rem(dp, 2)
+    z, y = fs // 2, lax.rem(fs, 2)
+    xn, cn, yn = 1 - x, 1 - c, 1 - y
+    NZ = 4
+    NE = 4
+    CAP = 160
+    D = 768
+
+    def at(xx, cc, zz, yy):
+        return (xx * 2 + cc, zz * 2 + yy)
+
+    core_d, x_d, y_d = at(x, cn, z, y), at(xn, c, z, y), at(x, c, z, yn)
+
+    def zz_of(step):
+        return lax.rem(z + step, NZ)
+
+    def z_d(step):
+        return at(x, c, zz_of(step), y)
+
+    def remote(src, dst, ss, rs, where):
+        return pltpu.make_async_remote_copy(
+            src_ref=src, dst_ref=dst, send_sem=ss, recv_sem=rs, device_id=where, device_id_type=MESH
+        )
+
+    for s in range(3):
+        for half in range(2):
+            for k in range(3):
+                aq[dp, z, y, s, :, half * 384 + k * 128 : half * 384 + k * 128 + 128] = qshard[
+                    :, k * D + (2 * s + half) * 128 : k * D + (2 * s + half) * 128 + 128
+                ]
+    ar[dp, z, y, :, :D] = oshard[...]
+    ar[dp, z, y, :, D:] = sshard[...]
+
+    barrier = pltpu.get_barrier_semaphore()
+    peers = [core_d, x_d, y_d, z_d(1), z_d(2), z_d(3)]
+    for peer in peers:
+        pl.semaphore_signal(barrier, inc=1, device_id=peer, device_id_type=MESH)
+    pl.semaphore_wait(barrier, len(peers))
+
+    def block(part, dpi, zi, yi):
+        return (aq if part == 0 else ar).at[dpi, zi, yi]
+
+    def s1(part, slot, dpi, zi, yi, where):
+        ref = block(part, dpi, zi, yi)
+        return remote(ref, ref, s1s.at[part, slot], s1r.at[part, dpi * 8 + zi * 2 + yi], where)
+
+    started = []
+
+    def go(copy):
+        copy.start()
+        started.append(copy)
+
+    dpx, dpc = xn * 2 + c, x * 2 + cn
+    for part in (0, 1):
+        for st in (1, 2, 3):
+            go(s1(part, st - 1, dp, z, y, z_d(st)))
+        go(s1(part, 3, dp, z, y, y_d))
+        go(s1(part, 7, dp, z, y, x_d))
+        go(s1(part, 15, dp, z, y, core_d))
+
+    route_v = routes[...]
+    live_v = valid[...] > 0
+    picks = jnp.where((iota((8, LONG), 0) == route_v) & live_v, 1.0, 0.0)
+    upto = jnp.where(iota((LONG, LONG), 0) <= iota((LONG, LONG), 1), 1.0, 0.0).astype(BF16)
+    counts = nn(picks.astype(BF16), upto)
+    place = jnp.sum(picks * counts, axis=0, keepdims=True).astype(jnp.int32) - 1
+    kept = live_v & (place < CAP)
+    code = jnp.where(kept, route_v * CAP + place, -1)
+    code_row[...] = code
+    keptf = jnp.where(kept, 1.0, 0.0)
+    sent = jnp.sum(picks * keptf, axis=1, keepdims=True)
+    lost = jnp.sum(picks * (1.0 - keptf), axis=1, keepdims=True)
+    lane128 = iota((8, 128), 1)
+    relg[3] = jnp.zeros((16, 256), F32)
+    relg[3, 0:8, 0:128] = jnp.where(lane128 == 64, sent, 0.0) + jnp.where(lane128 == 65, lost, 0.0)
+    stacked = jnp.concatenate(
+        [
+            jnp.broadcast_to(code.astype(F32), (8, LONG)),
+            jnp.broadcast_to(route_v.astype(F32), (8, LONG)),
+            jnp.zeros((112, LONG), F32),
+        ],
+        axis=0,
+    )
+    cols[...] = jnp.transpose(stacked)
+    same = (iota((8, LONG), 1) // 128 == iota((8, LONG), 0)) | (length[0] >= LONG)
+    key_mask[...] = jnp.where(same & live_v, 0.0, NEG)
+
+    for st in (1, 2, 3):
+        zi = zz_of(st)
+        for part in (0, 1):
+            s1(part, 0, dp, zi, y, y_d).wait_recv()
+            go(s1(part, 3 + st, dp, zi, y, y_d))
+            go(s1(part, 7 + st, dp, zi, y, x_d))
+            go(s1(part, 15 + st, dp, zi, y, core_d))
+
+    rel16 = jnp.concatenate([rel[...], jnp.zeros((4, BUCKETS), F32)], axis=0)
+
+    def bucket_hot(kind, axis):
+        shape = (BUCKETS, 256) if axis == 0 else (256, BUCKETS)
+        lane = iota(shape, 1 - axis)
+        offset = jnp.where(lane < 128, lane, lane - 256) + (0, 128, -128)[kind]
+        return jnp.where(bucket_of(offset) == iota(shape, axis), 1.0, 0.0)
+
+    rows_by_kind = [exact(rel16, bucket_hot(kind, 0), ((1,), (0,))) for kind in range(3)]
+    for b in (BUCKETS // 2 - 1, BUCKETS - 1):
+        rows_by_kind.append(exact(rel16, jnp.where(iota((BUCKETS, 256), 0) == b, 1.0, 0.0), ((1,), (0,))))
+    for head in range(HEADS):
+        for kind in range(5):
+            tab[head, kind : kind + 1, :] = rows_by_kind[kind][head : head + 1]
+
+    for st in range(4):
+        zi = zz_of(st)
+        for part in (0, 1):
+            s1(part, 0, dp, zi, yn, y_d).wait_recv()
+            go(s1(part, 11 + st, dp, zi, yn, x_d))
+            go(s1(part, 19 + st, dp, zi, yn, core_d))
+    for yi_off in range(2):
+        yi = y if yi_off == 0 else yn
+        for st in range(4):
+            zi = zz_of(st)
+            for part in (0, 1):
+                s1(part, 0, dpx, zi, yi, x_d).wait_recv()
+                go(s1(part, 23 + yi_off * 4 + st, dpx, zi, yi, core_d))
+    for dpi in (dpc, xn * 2 + cn):
+        for yi in range(2):
+            for zi in range(4):
+                for part in (0, 1):
+                    s1(part, 0, dpi, zi, yi, core_d).wait_recv()
+    for copy in started:
+        copy.wait_send()
+
+    def s3_src(m, e):
+        return (wi_hbm if m == 0 else wo_hbm).at[e]
+
+    def s3_z(m, e, st):
+        return remote(s3_src(m, e), wb.at[m, e, z, y], s3zs.at[m, e, st - 1], s3r.at[m, e, z, y], z_d(st))
+
+    def s3_own(m, e):
+        return pltpu.make_async_copy(s3_src(m, e), wb.at[m, e, z, y], s3l.at[m, e])
+
+    def s3_y0(m, e):
+        return remote(s3_src(m, e), wb.at[m, e, z, y], s3ys.at[m, e, 0], s3r.at[m, e, z, y], y_d)
+
+    def s3_y(m, e, st):
+        ref = wb.at[m, e, zz_of(st), y]
+        return remote(ref, ref, s3ys.at[m, e, st], s3r.at[m, e, zz_of(st), y], y_d)
+
+    def s3_arrival(m, e, zi, yi):
+        ref = wb.at[m, e, zi, yi]
+        return remote(ref, ref, s3ys.at[m, e, 0], s3r.at[m, e, zi, yi], y_d)
+
+    def s3_issue(e):
+        for m in range(2):
+            for st in (1, 2, 3):
+                s3_z(m, e, st).start()
+            s3_y0(m, e).start()
+            s3_own(m, e).start()
+
+    def s3_forward(m, e, st):
+        s3_arrival(m, e, zz_of(st), y).wait_recv()
+        s3_y(m, e, st).start()
+
+    def s3_finish(e):
+        for m in range(2):
+            s3_own(m, e).wait()
+            for st in range(4):
+                s3_arrival(m, e, zz_of(st), yn).wait_recv()
+
+    def s3_sent(e):
+        for m in range(2):
+            for st in (1, 2, 3):
+                s3_z(m, e, st).wait_send()
+                s3_y(m, e, st).wait_send()
+            s3_y0(m, e).wait_send()
+
+    s3_issue(0)
+    s3_issue(1)
+
+    @pl.loop(0, 4)
+    def _(dpi):
+        for zi in range(4):
+            base = pl.multiple_of((dpi * 8 + zi * 2) * 24, 16)
+            for s in range(3):
+                v = aq[dpi, zi, :, s].astype(F32).reshape(48, D)
+                wq[s, pl.ds(base, 48)] = v.astype(BF16)
+            v = ar[dpi, zi].astype(F32).reshape(48, 896)
+            wo[pl.ds(base, 48)] = v.astype(BF16)
+
+    for peer in peers:
+        pl.semaphore_signal(free, inc=1, device_id=peer, device_id_type=MESH)
+    sm_t[...] = jnp.transpose(wo[:, D:].astype(F32))
+    gain1 = sm_t[0:1, :]
+    gain2 = sm_t[1:2, :]
+
+    @pl.loop(0, 4)
+    def _(rb):
+        rows = pl.ds(pl.multiple_of(rb * 128, 128), 128)
+        xf = tok[rows].astype(F32)
+        r1 = lax.rsqrt(jnp.mean(xf * xf, axis=-1, keepdims=True) + EPS)
+        u1[rows] = (xf * r1 * gain1).astype(BF16)
+
+    for s in range(3):
+        qkvb[s] = nn(u1[...], wq[s]).astype(BF16)
+
+    lane_low = iota((LONG, 128), 1) < 64
+
+    def head_mask(v, h2):
+        return jnp.where(lane_low if h2 == 0 else ~lane_low, v, jnp.zeros((), v.dtype))
+
+    def p_copy(hp, out):
+        slot = lax.rem(hp, 2)
+        if out:
+            return pltpu.make_async_copy(pst.at[slot], p_hbm.at[hp], psem.at[slot])
+        return pltpu.make_async_copy(p_hbm.at[hp], pst.at[slot], psem.at[slot])
+
+    @pl.loop(0, HEADS // 2)
+    def _(hp):
+        slot = lax.rem(hp, 2)
+        s, base = hp // 2, pl.multiple_of(lax.rem(hp, 2) * 384, 128)
+        q2 = qkvb[s, :, pl.ds(base, 128)]
+        k2 = qkvb[s, :, pl.ds(base + 128, 128)]
+        v2 = qkvb[s, :, pl.ds(base + 256, 128)]
+
+        @pl.when(hp >= 2)
+        def _():
+            p_copy(hp, True).wait()
+
+        for h2 in range(2):
+            head = hp * 2 + h2
+            qm = head_mask(q2, h2) * jnp.asarray(0.125, BF16)
+            vm = head_mask(v2, h2)
+            for kind in range(3):
+                row = tab[head, kind : kind + 1, :]
+                tile = pltpu.roll(jnp.broadcast_to(row, (128, 256)), 0, 1, stride=1, stride_axis=0)
+                bias[kind] = tile[:, :128]
+            left = jnp.broadcast_to(tab[head, 3:4, 0:128], (128, 128))
+            right = jnp.broadcast_to(tab[head, 4:5, 0:128], (128, 128))
+            for bi in range(4):
+                rows = slice(bi * 128, bi * 128 + 128)
+                sc = nt(qm[rows], k2)
+                tiles = [
+                    bias[0] if bj == bi else bias[1] if bj == bi + 1 else bias[2] if bj == bi - 1
+                    else right if bj > bi else left
+                    for bj in range(4)
+                ]
+                sc = sc + jnp.concatenate(tiles, axis=1) + key_mask[bi : bi + 1, :]
+                peak = jnp.max(sc, axis=-1, keepdims=True)
+                ex = jnp.exp(sc - peak)
+                p = (ex * (1.0 / jnp.sum(ex, axis=-1, keepdims=True))).astype(BF16)
+                pst[slot, h2, rows] = p
+                part = nn(p, vm)
+                if h2 == 0:
+                    hid[rows, 0:128] = part
+                else:
+                    obuf[rows, pl.ds(pl.multiple_of(hp * 128, 128), 128)] = (
+                        hid[rows, 0:128] + part
+                    ).astype(BF16)
+        p_copy(hp, True).start()
+        s3_forward(hp // 3, 0, 1 + lax.rem(hp, 3))
+
+    s3_issue(2)
+
+    lane = iota((128, 128), 1)
+    is_logit = (lane >= 2) & (lane < 2 + NE)
+
+    def probs_of(logits):
+        lm = jnp.where(is_logit, logits, NEG)
+        ex = jnp.where(is_logit, jnp.exp(lm - jnp.max(lm, axis=-1, keepdims=True)), 0.0)
+        return ex / jnp.sum(ex, axis=-1, keepdims=True)
+
+    @pl.loop(0, 4)
+    def _(rb):
+        rows = pl.ds(pl.multiple_of(rb * 128, 128), 128)
+        h = tok[rows].astype(F32) + nn(obuf[rows], wo[:, :D])
+        hid[rows] = h
+        r2 = lax.rsqrt(jnp.mean(h * h, axis=-1, keepdims=True) + EPS)
+        u = (h * r2 * gain2).astype(BF16)
+        u2[rows] = u
+        pr = probs_of(nn(u, wo[:, D:]))
+        prob[rows] = pr
+        hot = (lane - 2) == cols[rows, 8:9].astype(jnp.int32)
+        gate = jnp.sum(jnp.where(hot, pr, 0.0), axis=-1, keepdims=True)
+        gobuf[rows] = (gate * cot[rows].astype(F32)).astype(BF16)
+
+    def xg_send(kind, e):
+        if kind == 0:
+            return remote(xg.at[dp, e], xg.at[dp, e], xs.at[0, e], xr.at[dp, e], x_d)
+        if kind == 1:
+            return remote(xg.at[dp, e], xg.at[dp, e], xs.at[1, e], xr.at[dp, e], core_d)
+        return remote(xg.at[dpx, e], xg.at[dpx, e], xs.at[2, e], xr.at[dpx, e], core_d)
+
+    def xg_arrival(dpi, e):
+        return remote(xg.at[dpi, e], xg.at[dpi, e], xs.at[0, e], xr.at[dpi, e], x_d)
+
+    for e in range(NE):
+        hot = jnp.where(iota((CAP, LONG), 0) + e * CAP == code_row[...], 1.0, 0.0).astype(BF16)
+        xg[dp, e, 0] = nn(hot, u2[...]).astype(BF16)
+        xg[dp, e, 1] = nn(hot, gobuf[...]).astype(BF16)
+        xg_send(0, e).start()
+        xg_send(1, e).start()
+
+    for m in range(2):
+        for st in (1, 2, 3):
+            s3_forward(m, 1, st)
+    s3_issue(3)
+
+    def yc_send(xi, e):
+        return remote(xg.at[xi * 2 + cn, e], ycore.at[xi, e], ycs.at[xi, e], ycr.at[xi, e], core_d)
+
+    def yx_send(e):
+        return remote(xg.at[dpx, e], yx.at[e], yxs.at[e], yxr.at[e], x_d)
+
+    def dy_send(m, e):
+        return remote(wb.at[m, e, :, yn], ry.at[m, e], dys.at[m, e], dyr.at[m, e], y_d)
+
+    def dz_send(m, e, st):
+        return remote(
+            wb.at[m, e, zz_of(st), y], rz.at[m, e, st - 1], dzs.at[m, e, st - 1], dzr.at[m, e, st - 1], z_d(st)
+        )
+
+    def sum_x(e):
+        for xi in range(2):
+            yc_send(xi, e).wait_recv()
+        xg[dpx, e] = (xg[dpx, e].astype(F32) + ycore[xn, e].astype(F32)).astype(BF16)
+        yx_send(e).start()
+
+    def sum_z(e):
+        for m in range(2):
+            dy_send(m, e).wait_recv()
+            for st in (1, 2, 3, 0):
+                zi = zz_of(st)
+                wb[m, e, zi, y] = (wb[m, e, zi, y].astype(F32) + ry[m, e, zi].astype(F32)).astype(BF16)
+                if st:
+                    dz_send(m, e, st).start()
+
+    def fin_copy(number):
+        e, m = number // 2, number % 2
+        return pltpu.make_async_copy(fin.at[m], (wi_grad if m == 0 else wo_grad).at[e], fsem.at[m])
+
+    def grad_final(e):
+        for m in range(2):
+            total = wb[m, e, z, y].astype(F32)
+            for st in (1, 2, 3):
+                dz_send(m, e, st).wait_recv()
+                total = total + rz[m, e, st - 1].astype(F32)
+            number = e * 2 + m
+            if number >= 2:
+                fin_copy(number - 2).wait()
+            fin[m] = total
+            fin_copy(number).start()
+
+    def forward_x(e):
+        xg_arrival(dpx, e).wait_recv()
+        xg_send(2, e).start()
+
+    forward_x(0)
+    for e in range(NE):
+        xg_arrival(dpc, e).wait_recv()
+        xg_arrival(xn * 2 + cn, e).wait_recv()
+        s3_finish(e)
+        for kind in range(3):
+            xg_send(kind, e).wait_send()
+        s3_sent(e)
+        half = 4 * 96
+        for fc in range(2):
+            zs = slice(2 * fc, 2 * fc + 2)
+            xv = xg[:, e, 0].reshape(4 * CAP, D)
+            gv = xg[:, e, 1].reshape(4 * CAP, D)
+            wi_v = wb[0, e, zs].reshape(half, D)
+            wo_v = wb[1, e, zs].reshape(half, D)
+            zv = nt(xv, wi_v)
+            ga = nt(gv, wo_v)
+            t = jnp.tanh(GELU_C * (zv + 0.044715 * (zv * zv * zv)))
+            act = (0.5 * zv * (1.0 + t)).astype(BF16)
+            slope = 0.5 * (1.0 + t) + (0.5 * GELU_C) * zv * (1.0 - t * t) * (
+                1.0 + (3 * 0.044715) * (zv * zv)
+            )
+            gz = (ga * slope).astype(BF16)
+            if fc == 0:
+                yacc = nn(act, wo_v)
+                gacc = nn(gz, wi_v)
+                pst_y, pst_g = yacc, gacc
+            else:
+                pst_y = pst_y + nn(act, wo_v)
+                pst_g = pst_g + nn(gz, wi_v)
+            wb[1, e, zs] = tn(act, gv).astype(BF16).reshape(2, 2, 96, D)
+            wb[0, e, zs] = tn(gz, xv).astype(BF16).reshape(2, 2, 96, D)
+            if fc == 0 and e < NE - 1:
+                forward_x(e + 1)
+        xg[:, e, 0] = pst_y.astype(BF16).reshape(4, CAP, D)
+        xg[:, e, 1] = pst_g.astype(BF16).reshape(4, CAP, D)
+        for xi in range(2):
+            yc_send(xi, e).start()
+        for m in range(2):
+            dy_send(m, e).start()
+        if e < 2:
+            for m in range(2):
+                for st in (1, 2, 3):
+                    s3_forward(m, e + 2, st)
+        if e >= 1:
+            sum_x(e - 1)
+        if e >= 2:
+            sum_z(e - 2)
+    sum_x(NE - 1)
+
+    for e in range(NE):
+        yx_send(e).wait_recv()
+        xg[dp, e] = (xg[dp, e].astype(F32) + ycore[x, e].astype(F32) + yx[e].astype(F32)).astype(BF16)
+    gd[0:8] = jnp.zeros((8, D), F32)
+
+    @pl.loop(0, 4)
+    def _(rb):
+        rows = pl.ds(pl.multiple_of(rb * 128, 128), 128)
+        code_col = cols[rows, 0:1].astype(jnp.int32)
+        back = jnp.where(iota((128, NE * CAP), 1) == code_col, 1.0, 0.0).astype(BF16)
+        yt = nn(back, xg[dp, :, 0].reshape(NE * CAP, D))
+        gxt = nn(back, xg[dp, :, 1].reshape(NE * CAP, D))
+        h = hid[rows]
+        g = cot[rows].astype(F32)
+        pr = prob[rows]
+        hot = (lane - 2) == cols[rows, 8:9].astype(jnp.int32)
+        gate = jnp.sum(jnp.where(hot, pr, 0.0), axis=-1, keepdims=True)
+        layer_out[rows] = (h + gate * yt).astype(BF16)
+        ggate = jnp.sum(g * yt, axis=-1, keepdims=True)
+        dprob = jnp.where(hot, ggate, 0.0)
+        dlog = pr * (dprob - jnp.sum(pr * dprob, axis=-1, keepdims=True))
+        prob[rows] = dlog
+        hi = dlog.astype(BF16)
+        lo = (dlog - hi.astype(F32)).astype(BF16)
+        wr_t = sm_t[...].astype(BF16)
+        gu = gxt + nn(hi, wr_t) + nn(lo, wr_t)
+        r2 = lax.rsqrt(jnp.mean(h * h, axis=-1, keepdims=True) + EPS)
+        n2 = h * r2
+        gd[1:2] = gd[1:2] + jnp.sum(gu * n2, axis=0, keepdims=True)
+        mm = gu * gain2
+        gh = g + r2 * (mm - n2 * jnp.mean(mm * n2, axis=-1, keepdims=True))
+        hid[rows] = gh
+        ghb = gh.astype(BF16)
+        gobuf[rows] = nt(ghb, wo[:, :D]).astype(BF16)
+        tokens_grad[rows] = ghb
+
+    dlog = prob[...]
+    dlog_hi = dlog.astype(BF16)
+    router_part = tn(u2[...], dlog_hi) + tn(u2[...], (dlog - dlog_hi.astype(F32)).astype(BF16))
+
+    for e in range(NE):
+        for xi in range(2):
+            yc_send(xi, e).wait_send()
+        yx_send(e).wait_send()
+    pl.semaphore_wait(free, len(peers))
+
+    def pack(unit, lanes, width, value):
+        for d in range(32):
+            xg[d // 8, d % 8 // 2, d % 2, unit * 32 : unit * 32 + 24, lanes] = value[
+                24 * d : 24 * d + 24
+            ].astype(BF16)
+
+    def lands(unit):
+        if unit == 4:
+            return lsc, lsx, lsy, lsz
+        if unit == 3:
+            full = pl.ds(0, D)
+            return (
+                ar.at[0:2, :, :, :, full], ar.at[2, :, :, :, full],
+                ar.at[3, :, 0, :, full], ar.at[3, 0:3, 1, :, full],
+            )
+        return aq.at[0:2, :, :, unit], aq.at[2, :, :, unit], aq.at[3, :, 0, unit], aq.at[3, 0:3, 1, unit]
+
+    def part_ref(unit):
+        if unit == 4:
+            return smallp
+        return xg.at[:, :, :, pl.ds(unit * 32, 24), :]
+
+    def narrow(unit, v):
+        return v if unit == 4 else v.astype(BF16)
+
+    def rs_core(unit, xi):
+        return remote(
+            part_ref(unit).at[xi * 2 + cn], lands(unit)[0].at[xi], rcs.at[unit, xi], rcr.at[unit, xi], core_d
+        )
+
+    def rs_x(unit):
+        return remote(part_ref(unit).at[dpx], lands(unit)[1], rxs.at[unit], rxr.at[unit], x_d)
+
+    def rs_y(unit):
+        return remote(part_ref(unit).at[dp, :, yn], lands(unit)[2], rys.at[unit], ryr.at[unit], y_d)
+
+    def rs_z(unit, st):
+        dst = lands(unit)[3].at[z] if unit == 4 else lands(unit)[3].at[st - 1]
+        return remote(
+            part_ref(unit).at[dp, zz_of(st), y], dst, rzs.at[unit, st - 1], rzr.at[unit, st - 1], z_d(st)
+        )
+
+    def st_core(unit):
+        for xi in range(2):
+            rs_core(unit, xi).start()
+
+    def st_x(unit):
+        mine, (lc, _, _, _) = part_ref(unit), lands(unit)
+        for xi in range(2):
+            rs_core(unit, xi).wait_recv()
+        for zi in range(4):
+            mine[dpx, zi] = narrow(unit, mine[dpx, zi].astype(F32) + lc[xn, zi].astype(F32))
+        rs_x(unit).start()
+
+    def st_y(unit):
+        mine, (lc, lx, _, _) = part_ref(unit), lands(unit)
+        rs_x(unit).wait_recv()
+        for zi in range(4):
+            mine[dp, zi] = narrow(
+                unit, mine[dp, zi].astype(F32) + lc[x, zi].astype(F32) + lx[zi].astype(F32)
+            )
+        rs_y(unit).start()
+
+    def st_z(unit):
+        mine, (_, _, ly, _) = part_ref(unit), lands(unit)
+        rs_y(unit).wait_recv()
+        for zi in range(4):
+            mine[dp, zi, y] = narrow(unit, mine[dp, zi, y].astype(F32) + ly[zi].astype(F32))
+        for st in (1, 2, 3):
+            rs_z(unit, st).start()
+
+    def st_final(unit):
+        mine, (_, _, _, lz) = part_ref(unit), lands(unit)
+        for st in (1, 2, 3):
+            rs_z(unit, st).wait_recv()
+        if unit == 4:
+            lz[z] = mine[dp, z, y]
+            return (lz[0] + lz[1]) + (lz[2] + lz[3])
+        total = mine[dp, z, y].astype(F32)
+        for st in (1, 2, 3):
+            total = total + lz[st - 1].astype(F32)
+        return total
+
+    def st_sent(unit):
+        for xi in range(2):
+            rs_core(unit, xi).wait_send()
+        rs_x(unit).wait_send()
+        rs_y(unit).wait_send()
+        for st in (1, 2, 3):
+            rs_z(unit, st).wait_send()
+
+    for half in range(2):
+        lanes = slice(half * 384, half * 384 + 384)
+        pack(3, lanes, 384, tn(obuf[...], tokens_grad[:, lanes]))
+    st_core(3)
+    sum_z(2)
+
+    relg[0] = jnp.zeros((16, 256), F32)
+    relg[1] = jnp.zeros((16, 256), F32)
+    relg[2] = jnp.zeros((16, 256), F32)
+    p_copy(4, True).wait()
+    p_copy(5, True).wait()
+    p_copy(0, False).start()
+
+    def backward(hp):
+        slot = hp % 2
+        s, base = hp // 2, (hp % 2) * 384
+        p_copy(hp, False).wait()
+        if hp < 5:
+            p_copy(hp + 1, False).start()
+        q2 = qkvb[s, :, base : base + 128]
+        k2 = qkvb[s, :, base + 128 : base + 256]
+        v2 = qkvb[s, :, base + 256 : base + 384]
+        go2 = gobuf[:, hp * 128 : hp * 128 + 128]
+        eighth = jnp.asarray(0.125, BF16)
+        for h2 in range(2):
+            head = hp * 2 + h2
+            qm = head_mask(q2, h2) * eighth
+            km = head_mask(k2, h2) * eighth
+            gm = head_mask(go2, h2)
+            tiles = [None] * 5
+            for bi in range(4):
+                rows = slice(bi * 128, bi * 128 + 128)
+                pv = pst[slot, h2, rows].astype(F32)
+                dpv = nt(gm[rows], v2)
+                ds = pv * (dpv - jnp.sum(pv * dpv, axis=-1, keepdims=True))
+                dst_s[rows] = ds.astype(BF16)
+                for bj in range(4):
+                    kind = 0 if bj == bi else 1 if bj == bi + 1 else 2 if bj == bi - 1 else 4 if bj > bi else 3
+                    tile = ds[:, bj * 128 : bj * 128 + 128]
+                    tiles[kind] = tile if tiles[kind] is None else tiles[kind] + tile
+            for kind in range(3):
+                relg[kind, head : head + 1, :] = diagonal_sums(tiles[kind])
+            relg[3, head : head + 1, 128:256] = jnp.sum(tiles[3], axis=0, keepdims=True)
+            relg[4, head : head + 1, 0:128] = jnp.sum(tiles[4], axis=0, keepdims=True)
+            dsb = dst_s[...]
+            dq = nn(dsb, km)
+            dk = tn(dsb, qm)
+            dv = tn(pst[slot, h2], gm)
+            if h2 == 0:
+                grad3 = [dq, dk, dv]
+            else:
+                grad3 = [a + b for a, b in zip(grad3, (dq, dk, dv))]
+        for k in range(3):
+            qkvb[s, :, base + k * 128 : base + k * 128 + 128] = grad3[k].astype(BF16)
+        pack(s, slice(base, base + 384), 384, tn(u1[...], qkvb[s, :, base : base + 384]))
+
+    backward(0)
+    st_x(3)
+    backward(1)
+    st_core(0)
+    st_y(3)
+    sum_z(3)
+    backward(2)
+    st_x(0)
+    st_z(3)
+    backward(3)
+    st_core(1)
+    st_y(0)
+    backward(4)
+    st_x(1)
+    st_z(0)
+    backward(5)
+    st_core(2)
+    st_y(1)
+
+    @pl.loop(0, 4)
+    def _(rb):
+        rows = pl.ds(pl.multiple_of(rb * 128, 128), 128)
+        gu = nt(qkvb[0, rows], wq[0]) + nt(qkvb[1, rows], wq[1]) + nt(qkvb[2, rows], wq[2])
+        xf = tok[rows].astype(F32)
+        r1 = lax.rsqrt(jnp.mean(xf * xf, axis=-1, keepdims=True) + EPS)
+        n1 = xf * r1
+        gd[0:1] = gd[0:1] + jnp.sum(gu * n1, axis=0, keepdims=True)
+        mm = gu * gain1
+        grad = hid[rows] + r1 * (mm - n1 * jnp.mean(mm * n1, axis=-1, keepdims=True))
+        tokens_grad[rows] = grad.astype(BF16)
+
+    st_x(2)
+    st_z(1)
+
+    gains = jnp.concatenate([gd[0:8], jnp.zeros((120, D), F32)], axis=0)
+    gain_cols = jnp.transpose(gains)
+    lane768 = iota((D, 128), 1)
+    small_cols = jnp.where(lane768 < 2, gain_cols, jnp.where(lane768 < 2 + NE, router_part, 0.0))
+    table = jnp.zeros((16, BUCKETS), F32)
+    for kind in range(3):
+        table = table + exact(relg[kind], bucket_hot(kind, 1), ((1,), (0,)))
+    far_b = iota((128, BUCKETS), 1)
+    table = table + exact(
+        relg[3, :, 128:256], jnp.where(far_b == BUCKETS // 2 - 1, 1.0, 0.0), ((1,), (0,))
+    )
+    table = table + exact(relg[4, :, 0:128], jnp.where(far_b == BUCKETS - 1, 1.0, 0.0), ((1,), (0,)))
+    extra = jnp.concatenate(
+        [
+            jnp.zeros((16, 32), F32),
+            table,
+            relg[3, :, 64:128],
+        ],
+        axis=1,
+    )
+    extra = jnp.concatenate([extra, jnp.zeros((8, 128), F32)], axis=0)
+    for d in range(32):
+        smallp[d // 8, d % 8 // 2, d % 2] = small_cols[24 * d : 24 * d + 24] + extra
+    st_core(4)
+    st_y(2)
+    st_x(4)
+    grad_final(0)
+    grad_final(1)
+    st_z(2)
+    st_y(4)
+    grad_final(2)
+    out_grad[...] = st_final(3)
+    st_z(4)
+
+    def write_qkv(unit):
+        total = st_final(unit)
+        for half in range(2):
+            for k in range(3):
+                qkv_grad[:, k * D + (2 * unit + half) * 128 : k * D + (2 * unit + half) * 128 + 128] = total[
+                    :, half * 384 + k * 128 : half * 384 + k * 128 + 128
+                ]
+
+    write_qkv(0)
+    write_qkv(1)
+    grad_final(3)
+    write_qkv(2)
+    small_grad[...] = st_final(4)
+    fin_copy(2 * NE - 2).wait()
+    fin_copy(2 * NE - 1).wait()
+
+    for e in range(NE):
+        for m in range(2):
+            dy_send(m, e).wait_send()
+            for st in (1, 2, 3):
+                dz_send(m, e, st).wait_send()
+    for unit in range(5):
+        st_sent(unit)
+
+
+def fused(
+    tokens, bucket_len, valid, routes, attn_gain, qkv_weight, out_weight, rel, ffn_gain, router_weight,
+    w_in, w_out, cotangent,
+):
+    tok_n, D = tokens.shape
+    small = jnp.concatenate(
+        [attn_gain[:, None], ffn_gain[:, None], router_weight, jnp.zeros((attn_gain.shape[0], 122), BF16)], axis=1
+    )
+    vm = pl.BlockSpec(memory_space=pltpu.VMEM)
+    hbm = pl.BlockSpec(memory_space=pl.ANY)
+    sds = jax.ShapeDtypeStruct
+    V = pltpu.VMEM
+    sem = lambda *s: pltpu.SemaphoreType.DMA(s)
+    outs = pl.pallas_call(
+        layer_kernel,
+        out_shape=(
+            sds((512, 768), BF16), sds((512, 768), BF16), sds((24, 2304), F32), sds((24, 768), F32),
+            sds((24, 128), F32), sds((4, 96, 768), F32), sds((4, 96, 768), F32), sds((6, 2, 512, 512), BF16),
+        ),
+        in_specs=[vm, vm, vm, vm, pl.BlockSpec(memory_space=pltpu.SMEM), vm, vm, vm, vm, hbm, hbm],
+        out_specs=(vm,) * 5 + (hbm,) * 3,
+        scratch_shapes=[
+            V((4, 4, 2, 3, 24, 768), BF16),
+            V((4, 4, 2, 24, 896), BF16),
+            V((3, 768, 768), BF16),
+            V((768, 896), BF16),
+            V((128, 768), F32),
+            V((2, 4, 4, 2, 96, 768), BF16),
+            V((4, 4, 2, 160, 768), BF16),
+            V((2, 4, 2, 160, 768), BF16),
+            V((4, 2, 160, 768), BF16),
+            V((2, 4, 4, 96, 768), BF16),
+            V((2, 4, 3, 96, 768), BF16),
+            V((3, 512, 768), BF16),
+            V((512, 768), BF16),
+            V((512, 768), BF16),
+            V((512, 768), BF16),
+            V((512, 768), BF16),
+            V((512, 768), F32),
+            V((512, 128), F32),
+            V((1, 512), jnp.int32),
+            V((512, 128), F32),
+            V((8, 512), F32),
+            V((12, 8, 256), F32),
+            V((3, 128, 128), F32),
+            V((2, 2, 512, 512), BF16),
+            V((512, 512), BF16),
+            V((8, 768), F32),
+            V((5, 16, 256), F32),
+            V((4, 4, 2, 24, 128), F32),
+            V((2, 4, 2, 24, 128), F32),
+            V((4, 2, 24, 128), F32),
+            V((4, 24, 128), F32),
+            V((4, 24, 128), F32),
+            V((2, 96, 768), F32),
+            pltpu.SemaphoreType.REGULAR,
+            sem(2, 31), sem(2, 32), sem(2, 4, 3), sem(2, 4, 4), sem(2, 4, 4, 2), sem(2, 4),
+            sem(3, 4), sem(4, 4), sem(2, 4), sem(2, 4), sem(4), sem(4), sem(2, 4), sem(2, 4),
+            sem(2, 4, 3), sem(2, 4, 3),
+            sem(5, 2), sem(5, 2), sem(5), sem(5), sem(5), sem(5), sem(5, 3), sem(5, 4), sem(2), sem(2),
+        ],
+        compiler_params=pltpu.CompilerParams(
+            collective_id=0, has_side_effects=True, vmem_limit_bytes=VMEM_LIMIT
+        ),
+        cost_estimate=pl.CostEstimate(flops=40_000_000_000, bytes_accessed=30_000_000, transcendentals=8_000_000),
+    )(
+        tokens, cotangent, routes.reshape(1, tok_n), valid.reshape(1, tok_n), bucket_len, rel,
+        qkv_weight, out_weight, small, jnp.transpose(w_in, (1, 0, 2)), jnp.transpose(w_out, (1, 0, 2)),
+    )
+    lo, tg, qg, og, sg, wig, wog, _ = outs
+    counts = sg[:4, 64:66].astype(jnp.int32)
+    return (
+        lo, tg, sg[:, 0], qg, og, sg[:12, 32:64], sg[:, 1], sg[:, 2:6],
+        jnp.transpose(wig, (1, 0, 2)), jnp.transpose(wog, (1, 0, 2)), counts[:, 0], counts[:, 1],
+    )
 
 
 epsilon = 1e-06
@@ -162,8 +1001,8 @@
         lax.all_gather(router_weight, ("dp", "fsdp"), axis=0, tiled=True),
     )
     expert_in, expert_out = (
-        lax.all_gather(w_in, ("dp", "fsdp"), axis=0, tiled=True),
-        lax.all_gather(w_out, ("dp", "fsdp"), axis=0, tiled=True),
+        lax.all_gather(w_in, "fsdp", axis=0, tiled=True),
+        lax.all_gather(w_out, "fsdp", axis=0, tiled=True),
     )
     token_count, model_width = tokens.shape
     block_total = token_count // LONG
@@ -218,12 +1057,18 @@
     slot_rows = jnp.where(
         slot_filled[:, None], normed_two_low[slot_token], jnp.zeros((), jnp.bfloat16)
     ).reshape(expert_count, capacity, model_width)
+    slot_rows = lax.all_gather(slot_rows, "dp", axis=1, tiled=True)
     expert_inner = jnp.einsum(
         "ecd,fed->ecf", slot_rows, expert_in, preferred_element_type=jnp.float32
     )
     active_low = jax.nn.gelu(expert_inner, approximate=True).astype(jnp.bfloat16)
     result_low = (
-        jnp.einsum("ecf,fed->ecd", active_low, expert_out, preferred_element_type=jnp.float32)
+        lax.psum_scatter(
+            jnp.einsum("ecf,fed->ecd", active_low, expert_out, preferred_element_type=jnp.float32),
+            "dp",
+            scatter_dimension=1,
+            tiled=True,
+        )
         .astype(jnp.bfloat16)
         .reshape(expert_count * capacity, model_width)
     )
@@ -232,17 +1077,6 @@
     sent_local = jnp.sum((route_picks & kept_rows[:, None]).astype(jnp.int32), axis=0)
     lost_local = jnp.sum((route_picks & ~kept_rows[:, None]).astype(jnp.int32), axis=0)
     count_sums = lax.psum(jnp.stack([sent_local, lost_local]), ("dp", "fsdp"))
-    gain_attn, weight_qkv, weight_out, gain_ffn, weight_router = (
-        lax.all_gather(attn_gain, ("dp", "fsdp"), axis=0, tiled=True),
-        lax.all_gather(qkv_weight, ("dp", "fsdp"), axis=0, tiled=True),
-        lax.all_gather(out_weight, ("dp", "fsdp"), axis=0, tiled=True),
-        lax.all_gather(ffn_gain, ("dp", "fsdp"), axis=0, tiled=True),
-        lax.all_gather(router_weight, ("dp", "fsdp"), axis=0, tiled=True),
-    )
-    expert_in, expert_out = (
-        lax.all_gather(w_in, ("dp", "fsdp"), axis=0, tiled=True),
-        lax.all_gather(w_out, ("dp", "fsdp"), axis=0, tiled=True),
-    )
     grad_out = cotangent.astype(jnp.float32)
     grad_gate = jnp.sum(grad_out * returned, axis=1)
     grad_back = gate_value[:, None] * grad_out
@@ -251,13 +1085,17 @@
         .astype(jnp.bfloat16)
         .reshape(expert_count, capacity, model_width)
     )
+    grad_result = lax.all_gather(grad_result, "dp", axis=1, tiled=True)
     grad_active = jnp.einsum(
         "ecd,fed->ecf", grad_result, expert_out, preferred_element_type=jnp.float32
     )
     unused_value, gelu_pullback = jax.vjp(partial(jax.nn.gelu, approximate=True), expert_inner)
     grad_inner = gelu_pullback(grad_active)[0].astype(jnp.bfloat16)
-    grad_slots = jnp.einsum(
-        "ecf,fed->ecd", grad_inner, expert_in, preferred_element_type=jnp.float32
+    grad_slots = lax.psum_scatter(
+        jnp.einsum("ecf,fed->ecd", grad_inner, expert_in, preferred_element_type=jnp.float32),
+        "dp",
+        scatter_dimension=1,
+        tiled=True,
     ).reshape(expert_count * capacity, model_width)
     grad_normed_two = jnp.where(kept_rows[:, None], grad_slots[slot_code], 0.0)
     grad_probs = jnp.where(route_hot, grad_gate[:, None], 0.0)
@@ -309,19 +1147,13 @@
         "ecf,ecd->fed", active_low, grad_result, preferred_element_type=jnp.float32
     )
     in_term = jnp.einsum("ecd,ecf->fed", slot_rows, grad_inner, preferred_element_type=jnp.float32)
-    expert_summed = lax.psum_scatter(
-        jnp.concatenate([in_term, out_term], axis=1),
-        ("dp", "fsdp"),
-        scatter_dimension=0,
-        tiled=True,
-    )
+    w_in_grad = lax.psum_scatter(in_term, "fsdp", scatter_dimension=0, tiled=True)
+    w_out_grad = lax.psum_scatter(out_term, "fsdp", scatter_dimension=0, tiled=True)
     attn_gain_grad = layer_summed[:, 0]
     qkv_grad = layer_summed[:, 1 : 1 + 3 * model_width]
     out_grad = layer_summed[:, 1 + 3 * model_width : 1 + 4 * model_width]
     ffn_gain_grad = layer_summed[:, 1 + 4 * model_width]
     router_weight_gradient = layer_summed[:, 2 + 4 * model_width :]
-    w_in_grad = expert_summed[:, :expert_count]
-    w_out_grad = expert_summed[:, expert_count:]
     return (
         layer_out,
         tokens_grad,
@@ -339,38 +1171,19 @@
 
 
 def solution(mesh):
+    both = ("dp", "fsdp")
+    body = fused if (mesh.shape["dp"], mesh.shape["fsdp"]) == (4, 8) else per_device
     placed = (
-        P(("dp", "fsdp"), None),
-        P(("dp", "fsdp")),
-        P(("dp", "fsdp")),
-        P(("dp", "fsdp"), None),
-        P(("dp", "fsdp")),
-        P(("dp", "fsdp"), None),
-        P(("dp", "fsdp"), None),
-        P(),
-        P(("dp", "fsdp")),
-        P(("dp", "fsdp"), None),
-        P(("dp", "fsdp"), None, None),
-        P(("dp", "fsdp"), None, None),
-        P(("dp", "fsdp"), None),
+        P(both, None), P(both), P(both), P(both, None), P(both), P(both, None), P(both, None), P(), P(both),
+        P(both, None), P(both, None, None), P(both, None, None), P(both, None),
     )
     return jax.shard_map(
-        per_device,
+        body,
         mesh=mesh,
         in_specs=placed,
         out_specs=(
-            P(("dp", "fsdp"), None),
-            P(("dp", "fsdp"), None),
-            P(("dp", "fsdp")),
-            P(("dp", "fsdp"), None),
-            P(("dp", "fsdp"), None),
-            P(),
-            P(("dp", "fsdp")),
-            P(("dp", "fsdp"), None),
-            P(("dp", "fsdp"), None, None),
-            P(("dp", "fsdp"), None, None),
-            P(),
-            P(),
+            P(both, None), P(both, None), P(both), P(both, None), P(both, None), P(), P(both), P(both, None),
+            P(both, None, None), P(both, None, None), P(), P(),
         ),
         check_vma=False,
     )

time: 1380 us -> 351 us (0.25)
  waiting for transfers between devices: 862 us -> 0 us
  Pallas kernels: 0 us -> 325 us
  blocking collectives: 190 us -> 0 us
  matrix products: 172 us -> 0 us
  other arithmetic: 75.9 us -> 1.43 us
  local copies, waits for them, and re-layouts: 54.4 us -> 18.5 us
  between operations: 15.7 us -> 1.55 us
    reduce_scatter x1 -> x0, waiting for transfers between devices: 660 us -> none  [per_device(): lax.psum_scatter(jnp.concatenate([in_term, out_term], axis=1), ('dp', 'fs...]
    pallas_call x0 -> x1, Pallas kernels: none -> 325 us  [fused(): pl.pallas_call(layer_kernel, out_shape=(sds((512, 768), BF16), sds((512,...]
    all_gather x4 -> x0, waiting for transfers between devices: 187 us -> none  [the longest x1 114 us: per_device(): lax.all_gather(w_out, ('dp', 'fsdp'), axis=0, tiled=True)]
    dot_general x23 -> x0, matrix products: 172 us -> none  [the longest x1 17.7 us: per_device(): jnp.einsum('ecf,ecd->fed', active_low, grad_result, preferred_element_typ...]
    psum x2 -> x0, blocking collectives: 81.5 us -> none  [the longest x1 41.3 us: per_device(): count_sums = lax.psum(jnp.stack([sent_local, lost_local]), ('dp', 'fsdp'))]
    all_gather x1 -> x0, blocking collectives: 66.2 us -> none  [per_device(): lax.all_gather(router_weight, ('dp', 'fsdp'), axis=0, tiled=True)]
    concatenate x1, other arithmetic: 50.1 us -> 0.68 us  [fused(): jnp.concatenate([attn_gain[:, None], ffn_gain[:, None], router_weight, jn...]
    unnamed x1 -> x0, blocking collectives: 42.1 us -> none
  transfers between devices with their start and end apart: 6 -> 0, of which waited for: 4 -> 0; matrix products, arithmetic and copies ran while one was open for 13% -> 0% of each run, Pallas kernels for 0% -> 0%
where the time goes in v1:
time: 351 us; the launch traced here: 346 us
  Pallas kernels  325 us (93%)
  local copies, waits for them, and re-layouts  18.5 us (5%)
    pallas_call x1, Pallas kernels, fused(): pl.pallas_call(layer_kernel, out_shape=(sds((512, 768), BF16), sds((512,...  325 us
    unnamed x18, local copies, waits for them, and re-layouts  10.2 us

profile of v1, /device:TPU:0, one launch (start us, length us, event | category | flops | bytes accessed | tf_op | source)
XLA Modules:
  0.0 346.3 jit_solution(281479664587445289)
XLA Ops:
  1.3 0.1 pad.3.clone
  1.4 0.7 copy.33
  2.1 0.7 copy.34
  2.9 0.8 copy.35
  3.6 0.7 maximum_maximum_fusion.sshard
  4.3 2.4 copy_bitcast_fusion
  6.7 324.9 %shard_map.220 = (bf16[512,768]{1,0:T(8,128)(2,1)}, bf16[512,768]{1,0:T(8,128)(2,1)}, f32[24,2304]{1,0:T(8,128)}, f32[24,768]{1,0:T(8,128)}, f32[24,128]{1,0:T(8...) custom-call(bf16[512,768]{1,0:T(8,128)(2,1)} %tok.1, bf16[512,768]{1,0:T(8,128)(2,1)} %cot.1, ...), custom_call_target="tpu_custom_call" | custom-call | flops 40000000000 | bytes 30000000 | tf_op jit(solution)/shard_map/pallas_call | solution.py:790
  331.6 1.5 slice_reduce_fusion
  333.0 0.8 slice_convert_fusion
  333.8 0.7 slice_reduce_fusion.2
  334.5 1.4 slice.22
  335.9 0.8 slice.24
  336.6 0.7 copy.38
  337.3 3.1 copy.39
  340.4 0.0 copy-done
  340.4 1.8 copy.40
  342.2 0.0 copy-done.2
  342.2 0.9 copy.48
  343.1 0.5 copy-done.1
  343.6 0.9 copy.49
  344.5 0.3 copy-done.3
  344.8 0.7 copy.50
  345.5 0.0 copy-done.4
  345.5 0.6 copy.51
  (6 shorter events, 0.0 us)
Async XLA Ops:
  337.3 3.1 copy-start
  340.4 1.8 copy-start.2
  342.2 1.4 copy-start.1
  343.6 1.1 copy-start.3
  343.6 1.8 copy-start.4
